TPU v7x, 32 devices: a whole 2x2x4 slice. The times are simulated.
32 devices in a mesh: groups: 2 (over y), gy: 4 (over z), gz: 2 (over x), wa: 2 (over core).
Axes of the slice: x: 2, y: 2, z: 4, core: 2. Of those that a mesh axis runs over, the one named last changes fastest.
Arguments:
- velocity: bfloat16 [3, 2048, 8, 1024], P(None, ('groups', 'gy'), ('gz', 'wa')), parts along dimension 1, may hold values from -6 to 6
- line_matrix: bfloat16 [1024, 1024], replicated, may hold values from -1.5 to 1.5
Outputs:
- advanced: bfloat16 [3, 2048, 8, 1024], P(None, ('groups', 'gy'), ('gz', 'wa')), parts along dimension 1
There are 2 independent parts, one for each index of `groups`. A program takes and returns all parts, laid end to end along the dimension named above; an argument that names none is the same for every part. Nothing has to cross between parts.
All inputs are finite; a program needn't handle non-finite values.
Results may differ from a plain program's by a relative error of at most 0.0061.
Values may be sent and summed in bfloat16 or wider, within the bound.
A program may use at most 128 MiB of HBM per device.

v0:
```python
import jax
import jax.numpy as jnp
from jax import lax
from jax.sharding import PartitionSpec as P

STEPS = 2


courant = 0.2
z_viscous = 0.3


def padded_2(block, sides, width):
    for axis, dim in sides:
        count = lax.axis_size(axis)
        forward = [(i, i + 1) for i in range(count - 1)]
        forward.append((count - 1, 0))
        backward = [(target, source) for source, target in forward]
        low = lax.ppermute(
            lax.slice_in_dim(block, block.shape[dim] - width, None, axis=dim), axis, forward
        )
        high = lax.ppermute(lax.slice_in_dim(block, 0, width, axis=dim), axis, backward)
        block = jnp.concatenate([low, block, high], axis=dim)
    return block


def central(upper_one, lower_one, upper_two, lower_two):
    return (8.0 * (upper_one - lower_one) - (upper_two - lower_two)) / 12.0


def tendency(padded, line_dim, whole_dim):
    planes = padded.shape[2] - 4
    cells = padded.shape[line_dim] - 4

    def crop(line_shift, plane_shift):
        piece = lax.slice_in_dim(padded, line_shift, line_shift + cells, axis=line_dim)
        return lax.slice_in_dim(piece, plane_shift, plane_shift + planes, axis=2).astype(
            jnp.float32
        )

    center = crop(2, 2)
    line_grad = central(crop(3, 2), crop(1, 2), crop(4, 2), crop(0, 2))
    plane_grad = central(crop(2, 3), crop(2, 1), crop(2, 4), crop(2, 0))
    whole_grad = central(
        jnp.roll(center, -1, whole_dim),
        jnp.roll(center, 1, whole_dim),
        jnp.roll(center, -2, whole_dim),
        jnp.roll(center, 2, whole_dim),
    )
    x_grad, y_grad = (whole_grad, line_grad)
    advection = center[0] * x_grad + center[1] * y_grad + center[2] * plane_grad
    z_diffusion = crop(2, 3) - 2.0 * center + crop(2, 1)
    return (center - courant * advection + z_viscous * z_diffusion).astype(jnp.bfloat16)


def x_solve(values, matrix):
    return jnp.einsum("ij,ayzj->ayzi", matrix, values, preferred_element_type=jnp.float32).astype(
        jnp.bfloat16
    )


def y_solve(values, matrix):
    return jnp.einsum("ij,ajzx->aizx", matrix, values, preferred_element_type=jnp.float32).astype(
        jnp.bfloat16
    )


def body(velocity, line_matrix):
    devices = lax.axis_size("gy")

    def to_columns(values):
        comps, rows_here, planes, cells = values.shape
        width = cells // devices
        split = values.reshape(comps, rows_here, planes, devices, width)
        received = lax.all_to_all(split, "gy", split_axis=3, concat_axis=1, tiled=True)
        joined = received.reshape(received.shape[0], received.shape[1], planes, width)
        return y_solve(joined, line_matrix)

    def to_rows(values):
        comps, cells, planes, width = values.shape
        joined = lax.all_to_all(
            values.reshape(comps, cells, planes, 1, width),
            "gy",
            split_axis=1,
            concat_axis=3,
            tiled=True,
        )
        return joined.reshape(comps, cells // devices, planes, devices * width)

    current = velocity
    for step_index in range(STEPS):
        padded = padded_2(current, (("gy", 1), (("gz", "wa"), 2)), 2)
        forcing = tendency(padded, 1, 3)
        if step_index % 2 == 0:
            current = to_rows(to_columns(x_solve(forcing, line_matrix)))
        else:
            current = x_solve(to_rows(to_columns(forcing)), line_matrix)
    return current


def solution(mesh):
    return jax.shard_map(
        body,
        mesh=mesh,
        in_specs=(P(None, ("groups", "gy"), ("gz", "wa"), None), P()),
        out_specs=P(None, ("groups", "gy"), ("gz", "wa"), None),
        check_vma=False,
    )
```

profile of v0, /device:TPU:7, one launch (start us, length us, event | category | flops | bytes accessed | tf_op | source)
XLA Modules:
  0.0 685.1 jit_solution(7781200990500748297)
XLA Ops:
  2.3 2.1 collective-permute-start
  4.4 8.6 %copy.34 = bf16[3,256,2,1024]{1,3,2,0:T(8,128)(2,1)} copy(bf16[3,256,2,1024]{3,2,1,0:T(2,128)(2,1)} %param.2) | data formatting | bytes 6291456 | tf_op args[0]
  13.0 1.6 copy.37
  14.6 1.6 copy.36
  16.2 6.5 pad_maximum_fusion
  22.7 9.3 %copy.42 = bf16[3,260,2,1024]{3,2,1,0:T(2,128)(2,1)} copy(bf16[3,260,2,1024]{1,3,2,0:T(8,128)(2,1)} %pad_maximum_fusion) | data formatting | bytes 6389760 | tf_op jit(solution)/shard_map/concatenate | solution.py:23
  33.4 2.5 convert_element_type.82
  35.9 2.8 fusion.40
  38.7 5.6 fusion.61
  44.3 5.6 fusion.59
  50.0 50.5 %collective-permute-done.3 = bf16[3,260,2,1024]{3,2,1,0:T(2,128)(2,1)} collective-permute-done((bf16[3,260,2,1024]{3,2,1,0:T(2,128)(2,1)}, bf16[3,260,2,1024]{3,2,1,0:T(2,128)(2,1)}, u32[]{:S(2)}, u32[]{:S(2)}) %collective-permute-start.3) | collective-permute-done | bytes 3194912 | tf_op jit(solution)/shard_map/ppermute | solution.py:19
  100.5 9.2 %copy.45 = bf16[3,260,2,1024]{1,3,2,0:T(8,128)(2,1)} copy(bf16[3,260,2,1024]{3,2,1,0:T(2,128)(2,1)} %collective-permute-done.3) | data formatting | bytes 6389760 | tf_op jit(solution)/shard_map/ppermute | solution.py:19
  109.7 9.2 %copy.43 = bf16[3,260,2,1024]{1,3,2,0:T(8,128)(2,1)} copy(bf16[3,260,2,1024]{3,2,1,0:T(2,128)(2,1)} %collective-permute-done.2) | data formatting | bytes 6389760 | tf_op jit(solution)/shard_map/ppermute | solution.py:22
  118.9 34.8 %fusion.32 = bf16[3,256,2,1024]{3,1,2,0:T(8,128)(2,1)} fusion(f32[3,256,2,1]{1,3,2,0:T(1,128)S(1)} %get-tuple-element.28, f32[3,256,2,1023]{1,3,2,0:T(8,128)} %get-tuple-element.30, f32[3,256,2,1023]{1,3,2,0:T(8,128)} %get-tuple-element.29, f32[3,256,2,1]{1,3,2,0:T(1,128)S(1)} %get-tuple-element.27, f32[3,256,2,2]{1,3,2,0:T(2,128)S(1)} %get-tuple-element.24, ...), kind=kOutput, calls=%fused_computation.72 | convolution fusion | flops 3323461632 | bytes 58757120 | tf_op jit(solution)/shard_map/ij,ayzj->ayzi/dot_general | solution.py:57
  153.6 2.2 copy.75
  155.9 72.6 %all_to_all.60 = bf16[3,256,2,4,256]{4,1,2,0,3:T(8,128)(2,1)} all-to-all(bf16[3,256,2,4,256]{4,1,2,0,3:T(8,128)(2,1)S(1)} %bitcast.68), channel_id=1, replica_groups=mesh['groups'=2,'gy'=4,'gz'=2,'wa'=2] {'gy'}, dimensions={3} | all-to-all | bytes 6291456 | tf_op jit(solution)/shard_map/all_to_all | solution.py:75
  228.5 5.9 copy.50
  234.3 6.1 reshape.41
  240.4 6.7 convert_bitcast_fusion.1
  247.2 8.7 %copy.51 = bf16[3,1024,2,1,256]{4,2,0,3,1:T(2,128)(2,1)} copy(bf16[3,1024,2,1,256]{1,4,2,0,3:T(8,128)(2,1)} %convert_bitcast_fusion.1) | data formatting | bytes 6291456 | tf_op jit(solution)/shard_map/reshape | solution.py:82
  255.8 74.8 %all_to_all.61 = bf16[3,1024,2,1,256]{4,2,0,3,1:T(2,128)(2,1)} all-to-all(bf16[3,1024,2,1,256]{4,2,0,3,1:T(2,128)(2,1)} %copy.51), channel_id=1, replica_groups=mesh['groups'=2,'gy'=4,'gz'=2,'wa'=2] {'gy'}, dimensions={1} | all-to-all | bytes 6291456 | tf_op jit(solution)/shard_map/all_to_all | solution.py:81
  330.7 8.6 %copy.52 = bf16[3,4,256,2,1,256]{2,5,1,3,0,4:T(8,128)(2,1)} copy(bf16[3,4,256,2,1,256]{5,3,0,2,1,4:T(2,128)(2,1)} %bitcast.70) | data formatting | bytes 6291456 | tf_op jit(solution)/shard_map/all_to_all | solution.py:81
  339.3 4.1 fusion.52
  343.4 1.7 copy.53
  346.7 1.7 copy.55
  348.5 1.6 copy.54
  350.1 2.8 collective-permute-done.5
  354.5 6.5 pad_maximum_fusion.1
  361.0 9.3 %copy.59 = bf16[3,260,2,1024]{3,2,1,0:T(2,128)(2,1)} copy(bf16[3,260,2,1024]{1,3,2,0:T(8,128)(2,1)} %pad_maximum_fusion.1) | data formatting | bytes 6389760 | tf_op jit(solution)/shard_map/concatenate | solution.py:23
  370.3 6.7 collective-permute-start.7
  377.4 2.5 convert_element_type.95
  379.9 2.8 fusion.37
  382.8 5.6 fusion.56
  388.4 5.6 fusion.54
  394.0 51.1 %collective-permute-done.7 = bf16[3,260,2,1024]{3,2,1,0:T(2,128)(2,1)} collective-permute-done((bf16[3,260,2,1024]{3,2,1,0:T(2,128)(2,1)}, bf16[3,260,2,1024]{3,2,1,0:T(2,128)(2,1)}, u32[]{:S(2)}, u32[]{:S(2)}) %collective-permute-start.7) | collective-permute-done | bytes 3194912 | tf_op jit(solution)/shard_map/ppermute | solution.py:19
  445.1 9.2 %copy.62 = bf16[3,260,2,1024]{1,3,2,0:T(8,128)(2,1)} copy(bf16[3,260,2,1024]{3,2,1,0:T(2,128)(2,1)} %collective-permute-done.7) | data formatting | bytes 6389760 | tf_op jit(solution)/shard_map/ppermute | solution.py:19
  454.3 9.2 %copy.60 = bf16[3,260,2,1024]{1,3,2,0:T(8,128)(2,1)} copy(bf16[3,260,2,1024]{3,2,1,0:T(2,128)(2,1)} %collective-permute-done.6) | data formatting | bytes 6389760 | tf_op jit(solution)/shard_map/ppermute | solution.py:22
  463.5 31.5 %fusion.16 = bf16[3,256,2,1024]{1,3,2,0:T(8,128)(2,1)S(1)} fusion(f32[3,256,2,1]{1,3,2,0:T(1,128)S(1)} %get-tuple-element.18, f32[3,256,2,1023]{1,3,2,0:T(8,128)} %get-tuple-element.20, f32[3,256,2,1023]{1,3,2,0:T(8,128)} %get-tuple-element.19, f32[3,256,2,1]{1,3,2,0:T(1,128)S(1)} %get-tuple-element.17, f32[3,256,2,2]{1,3,2,0:T(2,128)S(1)} %get-tuple-element.14, ...), kind=kLoop, calls=%fused_computation.22 | loop fusion | flops 100663296 | bytes 56659968 | tf_op jit(solution)/shard_map/convert_element_type | solution.py:53
  495.3 69.6 %all_to_all.62 = bf16[3,256,2,4,256]{1,4,2,0,3:T(8,128)(2,1)S(1)} all-to-all(bf16[3,256,2,4,256]{1,4,2,0,3:T(8,128)(2,1)S(1)} %copy.65), channel_id=1, replica_groups=mesh['groups'=2,'gy'=4,'gz'=2,'wa'=2] {'gy'}, dimensions={3} | all-to-all | bytes 6291456 | tf_op jit(solution)/shard_map/all_to_all | solution.py:75
  564.9 4.1 copy.66
  569.0 6.1 reshape.45
  575.1 6.7 convert_bitcast_fusion
  581.8 8.7 %copy.67 = bf16[3,1024,2,1,256]{4,2,0,3,1:T(2,128)(2,1)} copy(bf16[3,1024,2,1,256]{1,4,2,0,3:T(8,128)(2,1)} %convert_bitcast_fusion) | data formatting | bytes 6291456 | tf_op jit(solution)/shard_map/reshape | solution.py:82
  590.5 73.7 %all_to_all.63 = bf16[3,1024,2,1,256]{4,2,0,3,1:T(2,128)(2,1)S(1)} all-to-all(bf16[3,1024,2,1,256]{4,2,0,3,1:T(2,128)(2,1)} %copy.67), channel_id=1, replica_groups=mesh['groups'=2,'gy'=4,'gz'=2,'wa'=2] {'gy'}, dimensions={1} | all-to-all | bytes 6291456 | tf_op jit(solution)/shard_map/all_to_all | solution.py:81
  664.3 4.1 copy.76
  668.4 6.1 reshape.47
  674.4 5.6 convolution_convert_fusion
  680.0 4.9 copy.69
  (24 shorter events, 7.6 us)
Async XLA Ops:
  0.0 118.9 %copy-start = (bf16[1024,1024]{1,0:T(8,128)(2,1)S(1)}, bf16[1024,1024]{1,0:T(8,128)(2,1)}, u32[]{:S(2)}) copy-start(bf16[1024,1024]{1,0:T(8,128)(2,1)} %param.3) | copy-start | bytes 6291460
  0.9 12.0 %collective-permute-start.1 = (bf16[3,2,2,1024]{3,2,1,0:T(2,128)(2,1)S(1)}, bf16[3,2,2,1024]{3,2,1,0:T(2,128)(2,1)S(1)}, u32[]{:S(2)}, u32[]{:S(2)}) collective-permute-start(bf16[3,2,2,1024]{3,2,1,0:T(2,128)(2,1)S(1)} %get-tuple-element.22), channel_id=1, source_target_pairs={{0,4},{4,8},{8,12},{12,0},{1,5},{5,9},{9,13},{13,1},{2,6},{6,10},{... | collective-permute-start | bytes 73736 | tf_op jit(solution)/shard_map/ppermute | solution.py:19
  2.3 12.3 %collective-permute-start = (bf16[3,2,2,1024]{3,2,1,0:T(2,128)(2,1)S(1)}, bf16[3,2,2,1024]{3,2,1,0:T(2,128)(2,1)S(1)}, u32[]{:S(2)}, u32[]{:S(2)}) collective-permute-start(bf16[3,2,2,1024]{3,2,1,0:T(2,128)(2,1)S(1)} %get-tuple-element.21), channel_id=1, source_target_pairs={{4,0},{8,4},{12,8},{0,12},{5,1},{9,5},{13,9},{1,13},{6,2},{10,6},{... | collective-permute-start | bytes 73736 | tf_op jit(solution)/shard_map/ppermute | solution.py:22
  31.9 3.9 copy-start.2
  31.9 68.5 %collective-permute-start.3 = (bf16[3,260,2,1024]{3,2,1,0:T(2,128)(2,1)}, bf16[3,260,2,1024]{3,2,1,0:T(2,128)(2,1)}, u32[]{:S(2)}, u32[]{:S(2)}) collective-permute-start(bf16[3,260,2,1024]{3,2,1,0:T(2,128)(2,1)} %copy.42), channel_id=1, source_target_pairs={{0,1},{1,2},{2,3},{3,0},{4,5},{5,6},{6,7},{7,4},{8,9},{9,10},{10,1... | collective-permute-start | bytes 9584648 | tf_op jit(solution)/shard_map/ppermute | solution.py:19
  33.2 76.5 %collective-permute-start.2 = (bf16[3,260,2,1024]{3,2,1,0:T(2,128)(2,1)}, bf16[3,260,2,1024]{3,2,1,0:T(2,128)(2,1)}, u32[]{:S(2)}, u32[]{:S(2)}) collective-permute-start(bf16[3,260,2,1024]{3,2,1,0:T(2,128)(2,1)} %copy.42), channel_id=1, source_target_pairs={{1,0},{2,1},{3,2},{0,3},{5,4},{6,5},{7,6},{4,7},{9,8},{10,9},{11,1... | collective-permute-start | bytes 9584648 | tf_op jit(solution)/shard_map/ppermute | solution.py:22
  345.1 3.4 collective-permute-start.4
  348.4 4.5 collective-permute-start.5
  370.3 9.6 %copy-start.1 = (bf16[3,4,256,2,1,256]{2,5,1,3,0,4:T(8,128)(2,1)S(1)}, bf16[3,4,256,2,1,256]{2,5,1,3,0,4:T(8,128)(2,1)}, u32[]{:S(2)}) copy-start(bf16[3,4,256,2,1,256]{2,5,1,3,0,4:T(8,128)(2,1)} %copy.52) | copy-start | bytes 9437188
  370.3 74.8 %collective-permute-start.7 = (bf16[3,260,2,1024]{3,2,1,0:T(2,128)(2,1)}, bf16[3,260,2,1024]{3,2,1,0:T(2,128)(2,1)}, u32[]{:S(2)}, u32[]{:S(2)}) collective-permute-start(bf16[3,260,2,1024]{3,2,1,0:T(2,128)(2,1)} %copy.59), channel_id=1, source_target_pairs={{0,1},{1,2},{2,3},{3,0},{4,5},{5,6},{6,7},{7,4},{8,9},{9,10},{10,1... | collective-permute-start | bytes 9584648 | tf_op jit(solution)/shard_map/ppermute | solution.py:19
  377.0 77.3 %collective-permute-start.6 = (bf16[3,260,2,1024]{3,2,1,0:T(2,128)(2,1)}, bf16[3,260,2,1024]{3,2,1,0:T(2,128)(2,1)}, u32[]{:S(2)}, u32[]{:S(2)}) collective-permute-start(bf16[3,260,2,1024]{3,2,1,0:T(2,128)(2,1)} %copy.59), channel_id=1, source_target_pairs={{1,0},{2,1},{3,2},{0,3},{5,4},{6,5},{7,6},{4,7},{9,8},{10,9},{11,1... | collective-permute-start | bytes 9584648 | tf_op jit(solution)/shard_map/ppermute | solution.py:22
where the time goes:
time: 691 us; the launch traced here: 685 us
  blocking collectives  291 us (42%)
  local copies, waits for them, and re-layouts  167 us (24%)
  waiting for transfers between devices  104 us (15%)
  other arithmetic  55.1 us (8%)
  matrix products  53.8 us (8%)
  starting transfers between devices  13.6 us (2%)
    all_to_all x2, blocking collectives, to_rows(): lax.all_to_all(values.reshape(comps, cells, planes, 1, width), 'gy', spli...  149 us
    all_to_all x2, blocking collectives, to_columns(): lax.all_to_all(split, 'gy', split_axis=3, concat_axis=1, tiled=True)  142 us
    ppermute x4, waiting for transfers between devices, padded_2(): lax.ppermute(lax.slice_in_dim(block, block.shape[dim] - width, None, axis...  104 us
    dot_general x2, matrix products, x_solve(): jnp.einsum('ij,ayzj->ayzi', matrix, values, preferred_element_type=jnp.fl...  40.4 us
    convert_element_type x1, other arithmetic, tendency(): (center - courant * advection + z_viscous * z_diffusion).astype(jnp.bfloa...  31.5 us
    ppermute x4, local copies, waits for them, and re-layouts, padded_2(): lax.ppermute(lax.slice_in_dim(block, block.shape[dim] - width, None, axis...  21.6 us
    ppermute x4, local copies, waits for them, and re-layouts, padded_2(): lax.ppermute(lax.slice_in_dim(block, 0, width, axis=dim), axis, backward)  21.5 us
    concatenate x2, local copies, waits for them, and re-layouts, padded_2(): block = jnp.concatenate([low, block, high], axis=dim)  18.6 us
  transfers between devices with their start and end apart: 8, of which 3 were waited for; matrix products, arithmetic and copies ran while one was open for 9% of the time, Pallas kernels for 0%

commit v1 on v0

--- a/solution.py
+++ b/solution.py
@@ -47,7 +47,7 @@
         jnp.roll(center, -2, whole_dim),
         jnp.roll(center, 2, whole_dim),
     )
-    x_grad, y_grad = (whole_grad, line_grad)
+    x_grad, y_grad = (whole_grad, line_grad) if line_dim == 1 else (line_grad, whole_grad)
     advection = center[0] * x_grad + center[1] * y_grad + center[2] * plane_grad
     z_diffusion = crop(2, 3) - 2.0 * center + crop(2, 1)
     return (center - courant * advection + z_viscous * z_diffusion).astype(jnp.bfloat16)
@@ -66,36 +66,20 @@
 
 
 def body(velocity, line_matrix):
-    devices = lax.axis_size("gy")
+    planes_axis = ("gz", "wa")
 
     def to_columns(values):
-        comps, rows_here, planes, cells = values.shape
-        width = cells // devices
-        split = values.reshape(comps, rows_here, planes, devices, width)
-        received = lax.all_to_all(split, "gy", split_axis=3, concat_axis=1, tiled=True)
-        joined = received.reshape(received.shape[0], received.shape[1], planes, width)
-        return y_solve(joined, line_matrix)
+        return lax.all_to_all(values, "gy", split_axis=3, concat_axis=1, tiled=True)
 
     def to_rows(values):
-        comps, cells, planes, width = values.shape
-        joined = lax.all_to_all(
-            values.reshape(comps, cells, planes, 1, width),
-            "gy",
-            split_axis=1,
-            concat_axis=3,
-            tiled=True,
-        )
-        return joined.reshape(comps, cells // devices, planes, devices * width)
+        return lax.all_to_all(values, "gy", split_axis=1, concat_axis=3, tiled=True)
 
-    current = velocity
-    for step_index in range(STEPS):
-        padded = padded_2(current, (("gy", 1), (("gz", "wa"), 2)), 2)
-        forcing = tendency(padded, 1, 3)
-        if step_index % 2 == 0:
-            current = to_rows(to_columns(x_solve(forcing, line_matrix)))
-        else:
-            current = x_solve(to_rows(to_columns(forcing)), line_matrix)
-    return current
+    padded = padded_2(velocity, ((planes_axis, 2), ("gy", 1)), 2)
+    forcing = tendency(padded, 1, 3)
+    current = y_solve(to_columns(x_solve(forcing, line_matrix)), line_matrix)
+    padded = padded_2(current, ((planes_axis, 2), ("gy", 3)), 2)
+    forcing = tendency(padded, 3, 1)
+    return x_solve(to_rows(y_solve(forcing, line_matrix)), line_matrix)
 
 
 def solution(mesh):

time: 691 us -> 539 us (0.78)
  the two profiles are of different devices: /device:TPU:7 before, /device:TPU:9 now
where the time goes in v1:
time: 539 us; the launch traced here: 529 us
  blocking collectives  147 us (27%)
  other arithmetic  145 us (27%)
  local copies, waits for them, and re-layouts  90.5 us (17%)
  waiting for transfers between devices  86.8 us (16%)
  matrix products  50.1 us (9%)
  starting transfers between devices  9.32 us (2%)
    convert_element_type x1, other arithmetic, tendency(): (center - courant * advection + z_viscous * z_diffusion).astype(jnp.bfloa...  132 us
    ppermute x4, waiting for transfers between devices, padded_2(): lax.ppermute(lax.slice_in_dim(block, 0, width, axis=dim), axis, backward)  80.6 us
    all_to_all x1, blocking collectives, to_rows(): return lax.all_to_all(values, 'gy', split_axis=1, concat_axis=3, tiled=True)  73.6 us
    all_to_all x1, blocking collectives, to_columns(): return lax.all_to_all(values, 'gy', split_axis=3, concat_axis=1, tiled=True)  73.4 us
    dot_general x2, matrix products, y_solve(): jnp.einsum('ij,ajzx->aizx', matrix, values, preferred_element_type=jnp.fl...  37.7 us
    slice x2, local copies, waits for them, and re-layouts, tendency(): jnp.roll(center, -1, whole_dim)  16.7 us
    slice x2, local copies, waits for them, and re-layouts, tendency(): jnp.roll(center, -2, whole_dim)  16.1 us
    convert_element_type x2, local copies, waits for them, and re-layouts, x_solve(): jnp.einsum('ij,ayzj->ayzi', matrix, values, preferred_element_type=jnp.fl...  13.5 us
  transfers between devices with their start and end apart: 8, of which 6 were waited for; matrix products, arithmetic and copies ran while one was open for 11% of the time, Pallas kernels for 0%

profile of v1, /device:TPU:9, one launch (start us, length us, event | category | flops | bytes accessed | tf_op | source)
XLA Modules:
  0.0 529.5 jit_solution(9783384437028620620)
XLA Ops:
  0.0 0.0 copy-start
  0.0 0.7 collective-permute-start.1
  0.7 1.2 collective-permute-start
  1.8 4.1 convert_element_type.82
  6.0 0.0 copy-done.1
  6.0 1.6 fusion.57
  7.5 5.1 fusion.38
  12.6 14.6 %fusion.56 = (f32[3,256,2,1022]{3,2,1,0:T(2,128)}, f32[3,256,2,1022]{3,2,1,0:T(2,128)}) fusion(bf16[3,256,2,1024]{3,2,1,0:T(2,128)(2,1)} %param.2), kind=kLoop, calls=%fused_computation.94 | loop fusion | bytes 25116672 | tf_op jit(solution)/shard_map/jit(_roll_static)/slice | solution.py:47
  27.2 14.8 %fusion.54 = (f32[3,256,2,1023]{3,2,1,0:T(2,128)}, f32[3,256,2,1023]{3,2,1,0:T(2,128)}) fusion(bf16[3,256,2,1024]{3,2,1,0:T(2,128)(2,1)} %param.2), kind=kLoop, calls=%fused_computation.92 | loop fusion | bytes 25141248 | tf_op jit(solution)/shard_map/jit(_roll_static)/slice | solution.py:45
  42.0 28.3 %collective-permute-done.1 = bf16[3,256,2,1024]{3,2,1,0:T(2,128)(2,1)} collective-permute-done((bf16[3,256,2,1024]{3,2,1,0:T(2,128)(2,1)}, bf16[3,256,2,1024]{3,2,1,0:T(2,128)(2,1)}, u32[]{:S(2)}, u32[]{:S(2)}) %collective-permute-start.1) | collective-permute-done | bytes 3145760 | tf_op jit(solution)/shard_map/ppermute | solution.py:22
  70.2 0.0 collective-permute-done
  70.2 1.0 pad_maximum_fusion.18
  71.2 0.2 collective-permute-start.2
  71.5 1.3 collective-permute-start.3
  72.8 0.0 copy-done.2
  72.8 1.9 fusion.55
  74.7 0.1 collective-permute-done.2
  74.8 3.4 collective-permute-done.3
  78.2 0.0 copy-done.4
  78.2 132.4 %fusion.23 = bf16[3,256,2,1024]{3,2,1,0:T(2,128)(2,1)} fusion(bf16[3,256,2,1024]{3,2,1,0:T(2,128)(2,1)} %collective-permute-done, bf16[3,256,2,1024]{3,2,1,0:T(2,128)(2,1)} %collective-permute-done.1, f32[3,256,2,1022]{3,2,1,0:T(2,128)} %get-tuple-element.28, f32[3,256,2,2]{3,2,1,0:T(2,128)S(1)} %copy-done.8, f32[3,256,2,2]{3,2,1,0:T(2,128)S(1)} %get-tuple-element.29, ...), kind=kLoop, calls=%fused_computation.33 | loop fusion | flops 113246208 | bytes 44187648 | tf_op jit(solution)/shard_map/convert_element_type | solution.py:53
  210.6 6.9 %fusion.28 = bf16[3,256,2,1024]{3,1,2,0:T(8,128)(2,1)} fusion(bf16[3,256,2,1024]{3,2,1,0:T(2,128)(2,1)} %fusion.23, bf16[1024,1024]{1,0:T(8,128)(2,1)S(1)} %copy-done), kind=kOutput, calls=%fused_computation.57 | convolution fusion | flops 3222798336 | bytes 8388608 | tf_op jit(solution)/shard_map/ij,ayzj->ayzi/dot_general | solution.py:57
  217.4 8.6 %copy.8 = bf16[3,256,2,1024]{1,2,0,3:T(2,128)(2,1)} copy(bf16[3,256,2,1024]{3,1,2,0:T(8,128)(2,1)} %fusion.28) | data formatting | bytes 6291456 | tf_op jit(solution)/shard_map/convert_element_type | solution.py:57
  226.1 73.4 %all_to_all.36 = bf16[3,256,2,1024]{1,2,0,3:T(2,128)(2,1)S(1)} all-to-all(bf16[3,256,2,1024]{1,2,0,3:T(2,128)(2,1)} %copy.8), channel_id=1, replica_groups=mesh['groups'=2,'gy'=4,'gz'=2,'wa'=2] {'gy'}, dimensions={3} | all-to-all | bytes 6291456 | tf_op jit(solution)/shard_map/all_to_all | solution.py:72
  299.4 4.1 copy.21
  303.5 6.1 %all_to_all.29 = bf16[3,1024,2,256]{1,3,2,0:T(8,128)(2,1)} reshape(bf16[3,4,256,2,256]{2,1,4,3,0:T(4,128)(2,1)} %bitcast.44) | data formatting | bytes 6291456 | tf_op jit(solution)/shard_map/all_to_all | solution.py:72
  309.6 5.4 %fusion.58 = (f32[3,1024,2,256]{1,3,2,0:T(8,128)S(1)}, bf16[3,1024,2,256]{1,3,2,0:T(8,128)(2,1)S(1)}) fusion(bf16[3,1024,2,256]{1,3,2,0:T(8,128)(2,1)} %all_to_all.29, bf16[1024,1024]{1,0:T(8,128)(2,1)S(1)} %copy-done), kind=kOutput, calls=%fused_computation.96 | convolution fusion | flops 3224371200 | bytes 14680064 | tf_op jit(solution)/shard_map/ij,ajzx->aizx/dot_general | solution.py:63
  315.0 2.5 collective-permute-start.5
  317.5 1.9 collective-permute-start.4
  319.4 1.1 fusion.52
  320.5 2.8 fusion.35
  323.3 6.3 %fusion.53 = (f32[3,1023,2,256]{1,3,2,0:T(8,128)}, f32[3,1023,2,256]{1,3,2,0:T(8,128)}) fusion(bf16[3,1024,2,256]{1,3,2,0:T(8,128)(2,1)S(1)} %get-tuple-element.32), kind=kLoop, calls=%fused_computation.91 | loop fusion | bytes 25141248 | tf_op jit(solution)/shard_map/jit(_roll_static)/slice | solution.py:46
  329.6 6.3 %fusion.51 = (f32[3,1022,2,256]{1,3,2,0:T(8,128)}, f32[3,1022,2,256]{1,3,2,0:T(8,128)}) fusion(bf16[3,1024,2,256]{1,3,2,0:T(8,128)(2,1)S(1)} %get-tuple-element.32), kind=kLoop, calls=%fused_computation.89 | loop fusion | bytes 25116672 | tf_op jit(solution)/shard_map/jit(_roll_static)/slice | solution.py:48
  335.9 52.1 %collective-permute-done.5 = bf16[3,1024,2,256]{1,3,2,0:T(8,128)(2,1)S(1)} collective-permute-done((bf16[3,1024,2,256]{1,3,2,0:T(8,128)(2,1)S(1)}, bf16[3,1024,2,256]{1,3,2,0:T(8,128)(2,1)S(1)}, u32[]{:S(2)}, u32[]{:S(2)}) %collective-permute-start.5) | collective-permute-done | bytes 3145760 | tf_op jit(solution)/shard_map/ppermute | solution.py:22
  387.9 0.0 collective-permute-done.4
  387.9 0.1 pad_maximum_fusion.21
  388.0 1.6 collective-permute-start.6
  389.6 0.0 collective-permute-start.7
  389.6 1.5 fusion.50
  391.1 0.0 copy-done.7
  391.1 0.2 collective-permute-done.6
  391.3 2.8 collective-permute-done.7
  394.1 32.3 %convert_bitcast_fusion = bf16[3,1024,2,256]{1,3,2,0:T(8,128)(2,1)} fusion(f32[3,1,2,256]{1,3,2,0:T(8,128)} %get-tuple-element.20, f32[3,1023,2,256]{1,3,2,0:T(8,128)} %get-tuple-element.22, f32[3,1023,2,256]{1,3,2,0:T(8,128)} %get-tuple-element.21, f32[3,1,2,256]{1,3,2,0:T(8,128)S(1)} %get-tuple-element.19, f32[3,2,2,256]{1,3,2,0:T(8,128)} %get-tuple-element.16, ...), kind=kOutput, calls=%fused_computation.54 | convolution fusion | flops 3336044544 | bytes 46284800 | tf_op jit(solution)/shard_map/ij,ajzx->aizx/dot_general | solution.py:63
  426.4 8.6 %copy.10 = bf16[3,1024,2,256]{3,2,0,1:T(2,128)(2,1)} copy(bf16[3,1024,2,256]{1,3,2,0:T(8,128)(2,1)} %convert_bitcast_fusion) | data formatting | bytes 6291456 | tf_op jit(solution)/shard_map/convert_element_type | solution.py:63
  435.0 73.6 %all_to_all.37 = bf16[3,1024,2,256]{3,2,0,1:T(2,128)(2,1)S(1)} all-to-all(bf16[3,1024,2,256]{3,2,0,1:T(2,128)(2,1)} %copy.10), channel_id=1, replica_groups=mesh['groups'=2,'gy'=4,'gz'=2,'wa'=2] {'gy'}, dimensions={1} | all-to-all | bytes 6291456 | tf_op jit(solution)/shard_map/all_to_all | solution.py:75
  508.6 4.1 copy.20
  512.7 6.1 %all_to_all.33 = bf16[3,256,2,1024]{3,1,2,0:T(8,128)(2,1)} reshape(bf16[3,256,2,4,256]{4,3,1,2,0:T(4,128)(2,1)} %bitcast.46) | data formatting | bytes 6291456 | tf_op jit(solution)/shard_map/all_to_all | solution.py:75
  518.8 5.6 %convolution_convert_fusion = bf16[3,256,2,1024]{3,1,2,0:T(8,128)(2,1)S(1)} fusion(bf16[3,256,2,1024]{3,1,2,0:T(8,128)(2,1)} %all_to_all.33, bf16[1024,1024]{1,0:T(8,128)(2,1)S(1)} %copy-done), kind=kOutput, calls=%fused_computation.58 | convolution fusion | flops 3222798336 | bytes 8388608 | tf_op jit(solution)/shard_map/ij,ayzj->ayzi/dot_general | solution.py:57
  524.4 4.9 copy.12
  (13 shorter events, 0.0 us)
Async XLA Ops:
  0.0 210.6 %copy-start = (bf16[1024,1024]{1,0:T(8,128)(2,1)S(1)}, bf16[1024,1024]{1,0:T(8,128)(2,1)}, u32[]{:S(2)}) copy-start(bf16[1024,1024]{1,0:T(8,128)(2,1)} %param.3) | copy-start | bytes 6291460
  0.0 6.0 %copy-start.1 = (bf16[3,256,2,1024]{3,2,1,0:T(2,128)(2,1)S(1)}, bf16[3,256,2,1024]{3,2,1,0:T(2,128)(2,1)}, u32[]{:S(2)}) copy-start(bf16[3,256,2,1024]{3,2,1,0:T(2,128)(2,1)} %param.2) | copy-start | bytes 9437188
  0.0 70.2 %collective-permute-start.1 = (bf16[3,256,2,1024]{3,2,1,0:T(2,128)(2,1)}, bf16[3,256,2,1024]{3,2,1,0:T(2,128)(2,1)}, u32[]{:S(2)}, u32[]{:S(2)}) collective-permute-start(bf16[3,256,2,1024]{3,2,1,0:T(2,128)(2,1)} %param.2), channel_id=1, source_target_pairs={{1,0},{2,1},{3,2},{0,3},{5,4},{6,5},{7,6},{4,7},{9,8},{10,9},{11,1... | collective-permute-start | bytes 9437192 | tf_op jit(solution)/shard_map/ppermute | solution.py:22
  0.7 69.6 %collective-permute-start = (bf16[3,256,2,1024]{3,2,1,0:T(2,128)(2,1)}, bf16[3,256,2,1024]{3,2,1,0:T(2,128)(2,1)}, u32[]{:S(2)}, u32[]{:S(2)}) collective-permute-start(bf16[3,256,2,1024]{3,2,1,0:T(2,128)(2,1)} %param.2), channel_id=1, source_target_pairs={{0,1},{1,2},{2,3},{3,0},{4,5},{5,6},{6,7},{7,4},{8,9},{9,10},{10,1... | collective-permute-start | bytes 9437192 | tf_op jit(solution)/shard_map/ppermute | solution.py:19
  42.0 30.8 %copy-start.2 = (bf16[3,256,2,1024]{3,2,1,0:T(2,128)(2,1)S(1)}, bf16[3,256,2,1024]{3,2,1,0:T(2,128)(2,1)}, u32[]{:S(2)}) copy-start(bf16[3,256,2,1024]{3,2,1,0:T(2,128)(2,1)} %param.2) | copy-start | bytes 9437188
  42.0 36.2 %copy-start.4 = (f32[3,256,2,1022]{3,2,1,0:T(2,128)S(1)}, f32[3,256,2,1022]{3,2,1,0:T(2,128)}, u32[]{:S(2)}) copy-start(f32[3,256,2,1022]{3,2,1,0:T(2,128)} %get-tuple-element.27) | copy-start | bytes 18837508
  42.0 36.2 %copy-start.5 = (f32[256,2,1024]{2,1,0:T(2,128)S(1)}, f32[256,2,1024]{2,1,0:T(2,128)}, u32[]{:S(2)}) copy-start(f32[256,2,1024]{2,1,0:T(2,128)} %get-tuple-element.12) | copy-start | bytes 6291460
  42.0 36.2 %copy-start.8 = (f32[3,256,2,2]{3,2,1,0:T(2,128)S(1)}, f32[3,256,2,2]{3,2,1,0:T(2,128)}, u32[]{:S(2)}) copy-start(f32[3,256,2,2]{3,2,1,0:T(2,128)} %get-tuple-element.30) | copy-start | bytes 36868
  71.2 3.5 collective-permute-start.2
  71.5 6.7 %collective-permute-start.3 = (bf16[3,2,6,1024]{3,2,1,0:T(8,128)(2,1)S(1)}, bf16[3,2,6,1024]{3,2,1,0:T(8,128)(2,1)S(1)}, u32[]{:S(2)}, u32[]{:S(2)}) collective-permute-start(bf16[3,2,6,1024]{3,2,1,0:T(8,128)(2,1)S(1)} %get-tuple-element.8), channel_id=1, source_target_pairs={{0,4},{4,8},{8,12},{12,0},{1,5},{5,9},{9,13},{13,1},{2,6},{6,10},{... | collective-permute-start | bytes 221192 | tf_op jit(solution)/shard_map/ppermute | solution.py:19
  315.0 74.6 %copy-start.3 = (bf16[3,1024,2,256]{1,3,2,0:T(8,128)(2,1)}, bf16[3,1024,2,256]{1,3,2,0:T(8,128)(2,1)S(1)}, u32[]{:S(2)}) copy-start(bf16[3,1024,2,256]{1,3,2,0:T(8,128)(2,1)S(1)} %get-tuple-element.32) | copy-start | bytes 9437188
  315.0 72.9 %collective-permute-start.5 = (bf16[3,1024,2,256]{1,3,2,0:T(8,128)(2,1)S(1)}, bf16[3,1024,2,256]{1,3,2,0:T(8,128)(2,1)S(1)}, u32[]{:S(2)}, u32[]{:S(2)}) collective-permute-start(bf16[3,1024,2,256]{1,3,2,0:T(8,128)(2,1)S(1)} %get-tuple-element.32), channel_id=1, source_target_pairs={{1,0},{2,1},{3,2},{0,3},{5,4},{6,5},{7,6},{4,7},{9,8},{10,9},{11,1... | collective-permute-start | bytes 9437192 | tf_op jit(solution)/shard_map/ppermute | solution.py:22
  317.5 70.4 %collective-permute-start.4 = (bf16[3,1024,2,256]{1,3,2,0:T(8,128)(2,1)S(1)}, bf16[3,1024,2,256]{1,3,2,0:T(8,128)(2,1)S(1)}, u32[]{:S(2)}, u32[]{:S(2)}) collective-permute-start(bf16[3,1024,2,256]{1,3,2,0:T(8,128)(2,1)S(1)} %get-tuple-element.32), channel_id=1, source_target_pairs={{0,1},{1,2},{2,3},{3,0},{4,5},{5,6},{6,7},{7,4},{8,9},{9,10},{10,1... | collective-permute-start | bytes 9437192 | tf_op jit(solution)/shard_map/ppermute | solution.py:19
  387.9 3.2 copy-start.6
  387.9 3.2 copy-start.7
  388.0 3.3 collective-permute-start.6
  389.6 4.4 collective-permute-start.7

commit v2 on v1

--- a/solution.py
+++ b/solution.py
@@ -1,6 +1,10 @@
+import functools
+
 import jax
 import jax.numpy as jnp
 from jax import lax
+from jax.experimental import pallas as pl
+from jax.experimental.pallas import tpu as pltpu
 from jax.sharding import PartitionSpec as P
 
 STEPS = 2
@@ -82,9 +86,417 @@
     return x_solve(to_rows(y_solve(forcing, line_matrix)), line_matrix)
 
 
+CHUNKS = 4
+HALO = 16
+LANES = 128
+MESH = pl.DeviceIdType.MESH
+
+
+def coefficient(shift):
+    near = jnp.where(shift == 1, 8.0, 0.0) + jnp.where(shift == -1, -8.0, 0.0)
+    far = jnp.where(shift == 2, -1.0, 0.0) + jnp.where(shift == -2, 1.0, 0.0)
+    return near + far
+
+
+def iota2(shape):
+    return lax.broadcasted_iota(jnp.int32, shape, 0), lax.broadcasted_iota(jnp.int32, shape, 1)
+
+
+def matmul(a, b):
+    return jnp.dot(a, b, preferred_element_type=jnp.float32)
+
+
+def matmul_nt(a, b):
+    return lax.dot_general(a, b, (((1,), (1,)), ((), ())), preferred_element_type=jnp.float32)
+
+
+def steps_kernel(
+    sizes,
+    v_ref,
+    m_ref,
+    out_ref,
+    ext,
+    zh,
+    mid,
+    col,
+    st,
+    sib,
+    hp,
+    hr,
+    f2,
+    mid2,
+    rx,
+    band,
+    wide,
+    frc,
+    dxb,
+    dyb,
+    load_sem,
+    y_send,
+    y_recv,
+    z_send,
+    z_recv,
+    a_send,
+    a_recv,
+    s_send,
+    s_recv,
+    h_send,
+    h_recv,
+    b_send,
+    b_recv,
+):
+    NQ, NX, NW = sizes
+    comps, planes, rows, cells = v_ref.shape
+    line = NQ * rows
+    depth = NW * planes
+    chunk = rows // CHUNKS
+    q, X, w = lax.axis_index("gy"), lax.axis_index("gz"), lax.axis_index("wa")
+    ring = NX * NW
+    zi = X * NW + w
+    blocks = NQ * NX
+    b = q * NX + X
+
+    def device(dq, dX, dw):
+        return {"gy": dq, "gz": dX, "wa": dw}
+
+    def remote(src, dst, send, recv, to):
+        return pltpu.make_async_remote_copy(
+            src_ref=src, dst_ref=dst, send_sem=send, recv_sem=recv, device_id=to, device_id_type=MESH
+        )
+
+    load = pltpu.make_async_copy(v_ref, ext.at[:, :, pl.ds(HALO, rows), :], load_sem)
+    load.start()
+    barrier = pltpu.get_barrier_semaphore()
+    for dq in range(NQ):
+        for dX in range(NX):
+            for dw in range(NW):
+                if dq or dX or dw:
+                    to = device(lax.rem(q + dq, NQ), lax.rem(X + dX, NX), lax.rem(w + dw, NW))
+                    pl.semaphore_signal(barrier, inc=1, device_id=to, device_id_type=MESH)
+    pl.semaphore_wait(barrier, NQ * NX * NW - 1)
+
+    y_copies = []
+    for side, (step, start, land) in enumerate(
+        ((1, rows - HALO, 0), (NQ - 1, 0, rows + HALO))
+    ):
+        y_copies.append(
+            remote(
+                v_ref.at[:, :, pl.ds(start, HALO), :],
+                ext.at[:, :, pl.ds(land, HALO), :],
+                y_send.at[side],
+                y_recv.at[side],
+                device(lax.rem(q + step, NQ), X, w),
+            )
+        )
+
+    def z_copy(side, k):
+        other = lax.rem(zi + (1, ring - 1)[side], ring)
+        at = pl.ds(pl.multiple_of(k * chunk, chunk), chunk)
+        return remote(
+            v_ref.at[:, :, at, :],
+            zh.at[side, :, :, at, :],
+            z_send.at[side, k],
+            z_recv.at[side, k],
+            device(q, other // NW, lax.rem(other, NW)),
+        )
+
+    for copy in y_copies:
+        copy.start()
+    for k in range(2):
+        for side in range(2):
+            z_copy(side, k).start()
+
+    i, j = iota2((cells, cells))
+    shift = i - j
+    shift = jnp.where(shift > cells // 2, shift - cells, shift)
+    shift = jnp.where(shift < -(cells // 2), shift + cells, shift)
+    band[...] = coefficient(shift).astype(jnp.bfloat16)
+    i, j = iota2((chunk, chunk + 2 * HALO))
+    local = coefficient(j - HALO - i).astype(jnp.bfloat16)
+
+    load.wait()
+    for copy in y_copies:
+        copy.wait()
+
+    def a_copy(k, dq, dX):
+        to_q, to_X = lax.rem(q + dq, NQ), lax.rem(X + dX, NX)
+        lanes = pl.ds(pl.multiple_of((to_q * NX + to_X) * LANES, LANES), LANES)
+        src = mid.at[:, :, pl.ds(pl.multiple_of(k * chunk, chunk), chunk), lanes]
+        at = pl.ds(pl.multiple_of(q * rows + k * chunk, chunk), chunk)
+        dst = col.at[:, pl.ds(w * planes, planes), at, :]
+        recv = a_recv.at[k, q * NW + w]
+        return (
+            lambda: remote(src, dst, a_send.at[k, dq * NX + dX], recv, device(to_q, to_X, X)),
+            lambda: pltpu.make_async_copy(src, dst, recv),
+        )
+
+    away = [(dq, dx) for dq in (2, 1, 3, 0) if dq < NQ for dx in range(2)]
+    away += [(dq, dx) for dq in range(4, NQ) for dx in range(2)]
+
+    def start_pair(pair, own):
+        if own is None:
+            pair[0]().start()
+        else:
+
+            @pl.when(own)
+            def _():
+                pair[1]().start()
+
+            @pl.when(jnp.logical_not(own))
+            def _():
+                pair[0]().start()
+
+    def end_send(pair, own):
+        if own is None:
+            pair[0]().wait_send()
+        else:
+
+            @pl.when(jnp.logical_not(own))
+            def _():
+                pair[0]().wait_send()
+
+    @pl.loop(0, CHUNKS)
+    def _(k):
+        for side in range(2):
+            z_copy(side, k).wait()
+
+        @pl.when(k + 2 < CHUNKS)
+        def _():
+            for side in range(2):
+                z_copy(side, k + 2).start()
+
+        r0 = pl.multiple_of(k * chunk, chunk)
+        here = pl.ds(r0, chunk)
+        inner = pl.ds(pl.multiple_of(r0 + HALO, HALO), chunk)
+        center = ext[:, :, inner, :].reshape(comps * planes * chunk, cells)
+        wide[...] = matmul(center, band[...])
+        for z in range(planes):
+            speed = [ext[c, z, inner, :].astype(jnp.float32) for c in range(comps)]
+            for c in range(comps):
+
+                def plane(at):
+                    if at < 0:
+                        return zh[0, c, at + planes, here, :].astype(jnp.float32)
+                    if at >= planes:
+                        return zh[1, c, at - planes, here, :].astype(jnp.float32)
+                    return ext[c, at, inner, :].astype(jnp.float32)
+
+                y_grad = matmul(local, ext[c, z, pl.ds(r0, chunk + 2 * HALO), :])
+                x_grad = wide[pl.ds((c * planes + z) * chunk, chunk), :]
+                up, down = plane(z + 1), plane(z - 1)
+                z_grad = 8.0 * (up - down) - (plane(z + 2) - plane(z - 2))
+                advection = speed[0] * x_grad + speed[1] * y_grad + speed[2] * z_grad
+                diffusion = up - 2.0 * speed[c] + down
+                frc[pl.ds((c * planes + z) * chunk, chunk), :] = (
+                    speed[c] - (courant / 12.0) * advection + z_viscous * diffusion
+                ).astype(jnp.bfloat16)
+        solved = matmul_nt(frc[...], m_ref[...]).astype(jnp.bfloat16)
+        mid[:, :, here, :] = solved.reshape(comps, planes, chunk, cells)
+        for dq, dX in away:
+            start_pair(a_copy(k, dq, dX), (w == X) if (dq, dX) == (0, 0) else None)
+
+    @pl.loop(0, CHUNKS)
+    def _(k):
+        for source in range(NQ * NW):
+            piece = col.at[:, pl.ds(0, planes), pl.ds(0, chunk), :]
+            pltpu.make_async_copy(piece, piece, a_recv.at[k, source]).wait()
+
+    tile = 256
+
+    def sibling(c):
+        return remote(
+            st.at[c], sib.at[c], s_send.at[c], s_recv.at[c], device(q, X, lax.rem(w + 1, NW))
+        )
+
+    @pl.loop(0, comps)
+    def _(c):
+        right = jnp.concatenate([col[c, z] for z in range(depth)], axis=1)
+        for r in range(line // tile):
+            at = pl.ds(r * tile, tile)
+            solved = matmul(m_ref[at, :], right).astype(jnp.bfloat16)
+            for z in range(depth):
+                st[c, z, at, :] = solved[:, z * LANES : (z + 1) * LANES]
+        sibling(c).start()
+
+    picks = []
+    for z in range(comps * depth):
+        i, j = iota2((LANES, 2 * LANES))
+        right_edge = (i >= LANES - 2) & (j - 4 * z == i - (LANES - 2))
+        left_edge = (i < 2) & (j - LANES - 4 * z == i + 2)
+        picks.append(jnp.where(right_edge | left_edge, 1.0, 0.0).astype(jnp.bfloat16))
+    pick = jnp.concatenate(picks, axis=0)
+    for r in range(line // tile):
+        at = pl.ds(r * tile, tile)
+        left = jnp.concatenate(
+            [st[c, z, at, :] for c in range(comps) for z in range(depth)], axis=1
+        )
+        packed = matmul(left, pick).astype(jnp.bfloat16)
+        hp[0, at, :] = packed[:, :LANES]
+        hp[1, at, :] = packed[:, LANES:]
+    h_copies = []
+    for side, step in enumerate((1, blocks - 1)):
+        to = lax.rem(b + step, blocks)
+        h_copies.append(
+            remote(
+                hp.at[side],
+                hr.at[side],
+                h_send.at[side],
+                h_recv.at[side],
+                device(to // NX, lax.rem(to, NX), w),
+            )
+        )
+    for copy in h_copies:
+        copy.start()
+    for copy in h_copies:
+        copy.wait()
+    for c in range(comps):
+        sibling(c).wait()
+    hp[0] = hr[0] + hr[1]
+
+    def b_copy(c, dq, dw):
+        to_q, to_w = lax.rem(q + dq, NQ), lax.rem(w + dw, NW)
+        at = pl.ds(pl.multiple_of(to_q * rows, rows), rows)
+        src = mid2.at[c, pl.ds(to_w * planes, planes), at, :]
+        dst = rx.at[c, :, :, pl.ds(pl.multiple_of(b * LANES, LANES), LANES)]
+        recv = b_recv.at[c, b]
+        return (
+            lambda: remote(src, dst, b_send.at[c, dq * NW + dw], recv, device(to_q, w, to_w)),
+            lambda: pltpu.make_async_copy(src, dst, recv),
+        )
+
+    @pl.loop(0, comps)
+    def _(c):
+        right = jnp.concatenate([st[c, z] for z in range(depth)], axis=1)
+        for r in range(line // tile):
+            at = pl.ds(r * tile, tile)
+            dyb[at, :] = matmul(band[at, :], right)
+        for z in range(depth):
+            i, j = iota2((2 * LANES, LANES))
+            k = i - LANES - 4 * (c * depth + z)
+            edge = jnp.where(k < 2, k - 2, k - 2 + LANES)
+            place = jnp.where(i < LANES, i, edge)
+            used = (i < LANES) | ((k >= 0) & (k < 4))
+            weights = jnp.where(used, coefficient(place - j), 0.0).astype(jnp.bfloat16)
+            both = jnp.concatenate([st[c, z], hp[0]], axis=1)
+            dxb[z] = matmul(both, weights)
+
+        @pl.loop(0, line // LANES)
+        def _(r):
+            at = pl.ds(pl.multiple_of(r * LANES, LANES), LANES)
+            own = [st[c, z, at, :].astype(jnp.float32) for z in range(depth)]
+            other = [sib[c, z, at, :].astype(jnp.float32) for z in range(depth)]
+            ringed = own + other
+            for z in range(depth):
+                speed = [st[a, z, at, :].astype(jnp.float32) for a in range(comps)]
+                up, down = ringed[z + 1], ringed[z - 1]
+                z_grad = 8.0 * (up - down) - (ringed[z + 2] - ringed[z - 2])
+                advection = (
+                    speed[0] * dxb[z, at, :]
+                    - speed[1] * dyb[at, z * LANES : (z + 1) * LANES]
+                    + speed[2] * z_grad
+                )
+                diffusion = up - 2.0 * own[z] + down
+                f2[c, z, at, :] = (
+                    own[z] - (courant / 12.0) * advection + z_viscous * diffusion
+                ).astype(jnp.bfloat16)
+
+        forced = jnp.concatenate([f2[c, z] for z in range(depth)], axis=1)
+        for r in range(line // tile):
+            at = pl.ds(r * tile, tile)
+            solved = matmul(m_ref[at, :], forced).astype(jnp.bfloat16)
+            for z in range(depth):
+                mid2[c, z, at, :] = solved[:, z * LANES : (z + 1) * LANES]
+        for dq, dw in away:
+            start_pair(b_copy(c, dq, dw), (w == X) if (dq, dw) == (0, 0) else None)
+
+    @pl.loop(0, CHUNKS)
+    def _(k):
+        for dq, dX in away:
+            end_send(a_copy(k, dq, dX), (w == X) if (dq, dX) == (0, 0) else None)
+
+    @pl.loop(0, comps)
+    def _(c):
+        for source in range(blocks):
+            piece = rx.at[c, :, :, pl.ds(0, LANES)]
+            pltpu.make_async_copy(piece, piece, b_recv.at[c, source]).wait()
+        for z in range(planes):
+            out_ref[c, z] = matmul_nt(rx[c, z], m_ref[...]).astype(jnp.bfloat16)
+        for dq, dw in away:
+            end_send(b_copy(c, dq, dw), (w == X) if (dq, dw) == (0, 0) else None)
+
+
+def in_one_kernel(sizes, velocity, line_matrix):
+    NQ, NX, NW = sizes
+    comps, rows, planes, cells = velocity.shape
+    line = NQ * rows
+    depth = NW * planes
+    chunk = rows // CHUNKS
+    bf16 = jnp.bfloat16
+    columns = pltpu.VMEM((comps, depth, line, LANES), bf16)
+    dma = pltpu.SemaphoreType.DMA
+    out = pl.pallas_call(
+        functools.partial(steps_kernel, sizes),
+        out_shape=jax.ShapeDtypeStruct((comps, planes, rows, cells), bf16),
+        in_specs=[
+            pl.BlockSpec(memory_space=pl.ANY),
+            pl.BlockSpec(memory_space=pltpu.VMEM),
+        ],
+        out_specs=pl.BlockSpec(memory_space=pltpu.VMEM),
+        scratch_shapes=[
+            pltpu.VMEM((comps, planes, rows + 2 * HALO, cells), bf16),
+            pltpu.VMEM((2, comps, planes, rows, cells), bf16),
+            pltpu.VMEM((comps, planes, rows, cells), bf16),
+            columns,
+            columns,
+            columns,
+            pltpu.VMEM((2, line, LANES), bf16),
+            pltpu.VMEM((2, line, LANES), bf16),
+            columns,
+            columns,
+            pltpu.VMEM((comps, planes, rows, cells), bf16),
+            pltpu.VMEM((cells, cells), bf16),
+            pltpu.VMEM((comps * planes * chunk, cells), jnp.float32),
+            pltpu.VMEM((comps * planes * chunk, cells), bf16),
+            pltpu.VMEM((depth, line, LANES), jnp.float32),
+            pltpu.VMEM((line, depth * LANES), jnp.float32),
+            dma,
+            dma((2,)),
+            dma((2,)),
+            dma((2, CHUNKS)),
+            dma((2, CHUNKS)),
+            dma((CHUNKS, NQ * NX)),
+            dma((CHUNKS, NQ * NW)),
+            dma((comps,)),
+            dma((comps,)),
+            dma((2,)),
+            dma((2,)),
+            dma((comps, NQ * NW)),
+            dma((comps, NQ * NX)),
+        ],
+        compiler_params=pltpu.CompilerParams(
+            collective_id=0, has_side_effects=True, vmem_limit_bytes=60 * 1024 * 1024
+        ),
+    )(jnp.transpose(velocity, (0, 2, 1, 3)), line_matrix)
+    return jnp.transpose(out, (0, 2, 1, 3))
+
+
+def fits(sizes, velocity):
+    NQ, NX, NW = sizes
+    comps, rows, planes, cells = velocity.shape
+    same = NX == 2 and NW == 2 and planes == 2 and cells == NQ * rows
+    return same and cells == NQ * NX * LANES and rows % (16 * CHUNKS) == 0 and NQ >= 2
+
+
+def whole(velocity, line_matrix):
+    sizes = tuple(lax.axis_size(axis) for axis in ("gy", "gz", "wa"))
+    if fits(sizes, velocity):
+        return in_one_kernel(sizes, velocity, line_matrix)
+    return body(velocity, line_matrix)
+
+
 def solution(mesh):
     return jax.shard_map(
-        body,
+        whole,
         mesh=mesh,
         in_specs=(P(None, ("groups", "gy"), ("gz", "wa"), None), P()),
         out_specs=P(None, ("groups", "gy"), ("gz", "wa"), None),

time: 539 us -> 221 us (0.41); the launches traced: 529 us -> 221 us
  Pallas kernels: 0 us -> 210 us
  blocking collectives: 147 us -> 0 us
  other arithmetic: 145 us -> 0 us
  waiting for transfers between devices: 86.8 us -> 0 us
  local copies, waits for them, and re-layouts: 90.5 us -> 11.3 us
  matrix products: 50.1 us -> 0 us
  starting transfers between devices: 9.32 us -> 0 us
    pallas_call x0 -> x1, Pallas kernels: none -> 210 us  [in_one_kernel(): pl.pallas_call(functools.partial(steps_kernel, sizes), out_shape=jax.Shap...]
    all_to_all x2 -> x0, blocking collectives: 147 us -> none  [the longest x1 73.6 us: to_rows(): return lax.all_to_all(values, 'gy', split_axis=1, concat_axis=3, tiled=True)]
    convert_element_type x2 -> x0, other arithmetic: 136 us -> none  [the longest x1 132 us: tendency(): (center - courant * advection + z_viscous * z_diffusion).astype(jnp.bfloa...]
    ppermute x8 -> x0, waiting for transfers between devices: 86.8 us -> none  [the longest x4 80.6 us: padded_2(): lax.ppermute(lax.slice_in_dim(block, 0, width, axis=dim), axis, backward)]
    dot_general x4 -> x0, matrix products: 50.1 us -> none  [the longest x2 37.7 us: y_solve(): jnp.einsum('ij,ajzx->aizx', matrix, values, preferred_element_type=jnp.fl...]
    slice x8 -> x0, local copies, waits for them, and re-layouts: 48 us -> none  [the longest x2 16.7 us: tendency(): jnp.roll(center, -1, whole_dim)]
    convert_element_type x3 -> x0, local copies, waits for them, and re-layouts: 22.1 us -> none  [the longest x2 13.5 us: x_solve(): jnp.einsum('ij,ayzj->ayzi', matrix, values, preferred_element_type=jnp.fl...]
    all_to_all x4 -> x0, local copies, waits for them, and re-layouts: 20.3 us -> none  [the longest x2 10.2 us: to_columns(): return lax.all_to_all(values, 'gy', split_axis=3, concat_axis=1, tiled=True)]
  transfers between devices with their start and end apart: 8 -> 0, of which waited for: 6 -> 0; matrix products, arithmetic and copies ran while one was open for 11% -> 0% of each run, Pallas kernels for 0% -> 0%
where the time goes in v2:
time: 221 us
  Pallas kernels  210 us (95%)
  local copies, waits for them, and re-layouts  11.3 us (5%)
    pallas_call x1, Pallas kernels, in_one_kernel(): pl.pallas_call(functools.partial(steps_kernel, sizes), out_shape=jax.Shap...  210 us
    transpose x1, local copies, waits for them, and re-layouts, in_one_kernel(): return jnp.transpose(out, (0, 2, 1, 3))  6.79 us
    unnamed x1, local copies, waits for them, and re-layouts  4.53 us

profile of v2, /device:TPU:9, one launch (start us, length us, event | category | flops | bytes accessed | tf_op | source)
XLA Modules:
  0.0 221.2 jit_solution(10702216203316327929)
XLA Ops:
  0.0 4.5 %copy.6 = bf16[3,256,2,1024]{3,1,2,0:T(8,128)(2,1)} copy(bf16[3,256,2,1024]{3,2,1,0:T(2,128)(2,1)} %param.2) | data formatting | bytes 6291456 | tf_op args[0]
  4.5 209.9 %shard_map.28 = bf16[3,2,256,1024]{3,2,1,0:T(8,128)(2,1)} custom-call(bf16[3,2,256,1024]{3,2,1,0:T(8,128)(2,1)} %bitcast.5, bf16[1024,1024]{1,0:T(8,128)(2,1)} %m_ref.1), custom_call_target="tpu_custom_call" | custom-call | tf_op jit(solution)/shard_map/pallas_call | solution.py:437
  214.4 6.8 %copy.4 = bf16[3,256,2,1024]{3,2,1,0:T(2,128)(2,1)} copy(bf16[3,256,2,1024]{3,1,2,0:T(8,128)(2,1)} %bitcast.4) | data formatting | bytes 6291456 | tf_op jit(solution)/shard_map/transpose | solution.py:480

commit v3 on v2

--- a/solution.py
+++ b/solution.py
@@ -116,7 +116,6 @@
     m_ref,
     out_ref,
     ext,
-    zh,
     mid,
     col,
     st,
@@ -134,8 +133,12 @@
     load_sem,
     y_send,
     y_recv,
-    z_send,
-    z_recv,
+    own_send,
+    own_recv,
+    x_send,
+    x_recv,
+    f_send,
+    f_recv,
     a_send,
     a_recv,
     s_send,
@@ -149,10 +152,13 @@
     comps, planes, rows, cells = v_ref.shape
     line = NQ * rows
     depth = NW * planes
-    chunk = rows // CHUNKS
+    half = rows // NX
+    chunk = half // CHUNKS
     q, X, w = lax.axis_index("gy"), lax.axis_index("gz"), lax.axis_index("wa")
-    ring = NX * NW
-    zi = X * NW + w
+    ring = depth * NW
+    mine = X * depth + w * planes
+    theirs = (1 - X) * depth + w * planes
+    twin = {"gy": q, "gz": X, "wa": 1 - w}
     blocks = NQ * NX
     b = q * NX + X
 
@@ -164,7 +170,10 @@
             src_ref=src, dst_ref=dst, send_sem=send, recv_sem=recv, device_id=to, device_id_type=MESH
         )
 
-    load = pltpu.make_async_copy(v_ref, ext.at[:, :, pl.ds(HALO, rows), :], load_sem)
+    kept = rows - half + HALO
+    own_src = v_ref.at[:, :, pl.ds(pl.multiple_of(X * (half - HALO), HALO), kept), :]
+    own_dst = ext.at[:, pl.ds(mine, planes), pl.ds(pl.multiple_of((1 - X) * HALO, HALO), kept), :]
+    load = pltpu.make_async_copy(own_src, own_dst, load_sem)
     load.start()
     barrier = pltpu.get_barrier_semaphore()
     for dq in range(NQ):
@@ -177,34 +186,48 @@
 
     y_copies = []
     for side, (step, start, land) in enumerate(
-        ((1, rows - HALO, 0), (NQ - 1, 0, rows + HALO))
+        ((1, rows - HALO, 0), (NQ - 1, 0, half + HALO))
     ):
         y_copies.append(
             remote(
                 v_ref.at[:, :, pl.ds(start, HALO), :],
-                ext.at[:, :, pl.ds(land, HALO), :],
+                ext.at[:, pl.ds(mine, planes), pl.ds(land, HALO), :],
                 y_send.at[side],
-                y_recv.at[side],
-                device(lax.rem(q + step, NQ), X, w),
+                y_recv.at[w],
+                device(lax.rem(q + step, NQ), side, X),
             )
         )
-
-    def z_copy(side, k):
-        other = lax.rem(zi + (1, ring - 1)[side], ring)
-        at = pl.ds(pl.multiple_of(k * chunk, chunk), chunk)
+    to_twin = remote(own_src, own_dst, own_send, own_recv, twin)
+
+    def part(half_at, k):
+        if isinstance(k, int) and k == 0:
+            return pl.multiple_of(HALO + half_at * (half - HALO), HALO), HALO
+        down = half - chunk * k
+        up = 2 * HALO + chunk * (k - 1)
+        return pl.multiple_of(up + half_at * (down - up), HALO), chunk
+
+    def x_copy(k):
+        at, count = part(1 - X, k)
+        start = pl.multiple_of(at - HALO + (1 - X) * half, HALO)
         return remote(
-            v_ref.at[:, :, at, :],
-            zh.at[side, :, :, at, :],
-            z_send.at[side, k],
-            z_recv.at[side, k],
-            device(q, other // NW, lax.rem(other, NW)),
-        )
-
+            v_ref.at[:, :, pl.ds(start, count), :],
+            ext.at[:, pl.ds(mine, planes), pl.ds(at, count), :],
+            x_send.at[k],
+            x_recv.at[k],
+            device(q, 1 - X, w),
+        )
+
+    def forward(k):
+        at, count = part(X, k)
+        piece = ext.at[:, pl.ds(theirs, planes), pl.ds(at, count), :]
+        return remote(piece, piece, f_send.at[k], f_recv.at[k], twin)
+
+    for k in range(2):
+        x_copy(k).start()
+    to_twin.start()
     for copy in y_copies:
         copy.start()
-    for k in range(2):
-        for side in range(2):
-            z_copy(side, k).start()
+    x_copy(2).start()
 
     i, j = iota2((cells, cells))
     shift = i - j
@@ -215,20 +238,25 @@
     local = coefficient(j - HALO - i).astype(jnp.bfloat16)
 
     load.wait()
-    for copy in y_copies:
-        copy.wait()
+    to_twin.wait()
+    for side, copy in enumerate(y_copies):
+        copy.wait_send()
+        piece = ext.at[:, pl.ds(0, planes), pl.ds(0, HALO), :]
+        pltpu.make_async_copy(piece, piece, y_recv.at[side]).wait()
+    x_copy(0).wait()
+    forward(0).start()
+    forward(0).wait()
 
     def a_copy(k, dq, dX):
         to_q, to_X = lax.rem(q + dq, NQ), lax.rem(X + dX, NX)
         lanes = pl.ds(pl.multiple_of((to_q * NX + to_X) * LANES, LANES), LANES)
         src = mid.at[:, :, pl.ds(pl.multiple_of(k * chunk, chunk), chunk), lanes]
-        at = pl.ds(pl.multiple_of(q * rows + k * chunk, chunk), chunk)
-        dst = col.at[:, pl.ds(w * planes, planes), at, :]
-        recv = a_recv.at[k, q * NW + w]
-        return (
-            lambda: remote(src, dst, a_send.at[k, dq * NX + dX], recv, device(to_q, to_X, X)),
-            lambda: pltpu.make_async_copy(src, dst, recv),
-        )
+        at = pl.ds(pl.multiple_of(q * rows + X * half + k * chunk, chunk), chunk)
+        dst = col.at[:, :, at, :]
+        recv = a_recv.at[k, q * NX + X]
+        if (dq, dX) == (0, 0):
+            return pltpu.make_async_copy(src, dst, recv)
+        return remote(src, dst, a_send.at[k, dq * NX + dX], recv, device(to_q, to_X, w))
 
     away = [(dq, dx) for dq in (2, 1, 3, 0) if dq < NQ for dx in range(2)]
     away += [(dq, dx) for dq in range(4, NQ) for dx in range(2)]
@@ -256,49 +284,48 @@
                 pair[0]().wait_send()
 
     @pl.loop(0, CHUNKS)
-    def _(k):
-        for side in range(2):
-            z_copy(side, k).wait()
-
-        @pl.when(k + 2 < CHUNKS)
+    def _(n):
+        x_copy(n + 1).wait()
+        forward(n + 1).start()
+
+        @pl.when(n + 2 < CHUNKS)
         def _():
-            for side in range(2):
-                z_copy(side, k + 2).start()
-
+            x_copy(n + 3).start()
+
+        forward(n + 1).wait()
+        k = n + X * (CHUNKS - 1 - 2 * n)
         r0 = pl.multiple_of(k * chunk, chunk)
         here = pl.ds(r0, chunk)
         inner = pl.ds(pl.multiple_of(r0 + HALO, HALO), chunk)
-        center = ext[:, :, inner, :].reshape(comps * planes * chunk, cells)
+        center = ext[:, pl.ds(w * depth, depth), inner, :].reshape(comps * depth * chunk, cells)
         wide[...] = matmul(center, band[...])
-        for z in range(planes):
-            speed = [ext[c, z, inner, :].astype(jnp.float32) for c in range(comps)]
+        for z in range(depth):
+            at = w * depth + z
+            speed = [ext[c, at, inner, :].astype(jnp.float32) for c in range(comps)]
             for c in range(comps):
 
-                def plane(at):
-                    if at < 0:
-                        return zh[0, c, at + planes, here, :].astype(jnp.float32)
-                    if at >= planes:
-                        return zh[1, c, at - planes, here, :].astype(jnp.float32)
-                    return ext[c, at, inner, :].astype(jnp.float32)
-
-                y_grad = matmul(local, ext[c, z, pl.ds(r0, chunk + 2 * HALO), :])
-                x_grad = wide[pl.ds((c * planes + z) * chunk, chunk), :]
-                up, down = plane(z + 1), plane(z - 1)
-                z_grad = 8.0 * (up - down) - (plane(z + 2) - plane(z - 2))
+                def plane(shift):
+                    return ext[c, lax.rem(at + shift + ring, ring), inner, :].astype(jnp.float32)
+
+                y_grad = matmul(local, ext[c, at, pl.ds(r0, chunk + 2 * HALO), :])
+                lines = pl.ds((c * depth + z) * chunk, chunk)
+                x_grad = wide[lines, :]
+                up, down = plane(1), plane(-1)
+                z_grad = 8.0 * (up - down) - (plane(2) - plane(-2))
                 advection = speed[0] * x_grad + speed[1] * y_grad + speed[2] * z_grad
                 diffusion = up - 2.0 * speed[c] + down
-                frc[pl.ds((c * planes + z) * chunk, chunk), :] = (
+                frc[lines, :] = (
                     speed[c] - (courant / 12.0) * advection + z_viscous * diffusion
                 ).astype(jnp.bfloat16)
         solved = matmul_nt(frc[...], m_ref[...]).astype(jnp.bfloat16)
-        mid[:, :, here, :] = solved.reshape(comps, planes, chunk, cells)
+        mid[:, :, here, :] = solved.reshape(comps, depth, chunk, cells)
         for dq, dX in away:
-            start_pair(a_copy(k, dq, dX), (w == X) if (dq, dX) == (0, 0) else None)
+            a_copy(k, dq, dX).start()
 
     @pl.loop(0, CHUNKS)
     def _(k):
-        for source in range(NQ * NW):
-            piece = col.at[:, pl.ds(0, planes), pl.ds(0, chunk), :]
+        for source in range(NQ * NX):
+            piece = col.at[:, :, pl.ds(0, chunk), :]
             pltpu.make_async_copy(piece, piece, a_recv.at[k, source]).wait()
 
     tile = 256
@@ -412,7 +439,8 @@
     @pl.loop(0, CHUNKS)
     def _(k):
         for dq, dX in away:
-            end_send(a_copy(k, dq, dX), (w == X) if (dq, dX) == (0, 0) else None)
+            if (dq, dX) != (0, 0):
+                a_copy(k, dq, dX).wait_send()
 
     @pl.loop(0, comps)
     def _(c):
@@ -430,7 +458,8 @@
     comps, rows, planes, cells = velocity.shape
     line = NQ * rows
     depth = NW * planes
-    chunk = rows // CHUNKS
+    half = rows // NX
+    chunk = half // CHUNKS
     bf16 = jnp.bfloat16
     columns = pltpu.VMEM((comps, depth, line, LANES), bf16)
     dma = pltpu.SemaphoreType.DMA
@@ -443,9 +472,8 @@
         ],
         out_specs=pl.BlockSpec(memory_space=pltpu.VMEM),
         scratch_shapes=[
-            pltpu.VMEM((comps, planes, rows + 2 * HALO, cells), bf16),
-            pltpu.VMEM((2, comps, planes, rows, cells), bf16),
-            pltpu.VMEM((comps, planes, rows, cells), bf16),
+            pltpu.VMEM((comps, NX * depth, half + 2 * HALO, cells), bf16),
+            pltpu.VMEM((comps, depth, half, cells), bf16),
             columns,
             columns,
             columns,
@@ -455,17 +483,21 @@
             columns,
             pltpu.VMEM((comps, planes, rows, cells), bf16),
             pltpu.VMEM((cells, cells), bf16),
-            pltpu.VMEM((comps * planes * chunk, cells), jnp.float32),
-            pltpu.VMEM((comps * planes * chunk, cells), bf16),
+            pltpu.VMEM((comps * depth * chunk, cells), jnp.float32),
+            pltpu.VMEM((comps * depth * chunk, cells), bf16),
             pltpu.VMEM((depth, line, LANES), jnp.float32),
             pltpu.VMEM((line, depth * LANES), jnp.float32),
             dma,
             dma((2,)),
             dma((2,)),
-            dma((2, CHUNKS)),
-            dma((2, CHUNKS)),
+            dma,
+            dma,
+            dma((CHUNKS + 1,)),
+            dma((CHUNKS + 1,)),
+            dma((CHUNKS + 1,)),
+            dma((CHUNKS + 1,)),
             dma((CHUNKS, NQ * NX)),
-            dma((CHUNKS, NQ * NW)),
+            dma((CHUNKS, NQ * NX)),
             dma((comps,)),
             dma((comps,)),
             dma((2,)),
@@ -484,7 +516,7 @@
     NQ, NX, NW = sizes
     comps, rows, planes, cells = velocity.shape
     same = NX == 2 and NW == 2 and planes == 2 and cells == NQ * rows
-    return same and cells == NQ * NX * LANES and rows % (16 * CHUNKS) == 0 and NQ >= 2
+    return same and cells == NQ * NX * LANES and rows % (32 * NX * CHUNKS) == 0 and NQ >= 2
 
 
 def whole(velocity, line_matrix):

time: 221 us -> 203 us (0.919)
  Pallas kernels: 210 us -> 191 us
    pallas_call x1, Pallas kernels: 210 us -> 191 us  [in_one_kernel(): pl.pallas_call(functools.partial(steps_kernel, sizes), out_shape=jax.Shap...]
where the time goes in v3:
time: 203 us; the launch traced here: 202 us
  Pallas kernels  191 us (94%)
  local copies, waits for them, and re-layouts  11.3 us (6%)
    pallas_call x1, Pallas kernels, in_one_kernel(): pl.pallas_call(functools.partial(steps_kernel, sizes), out_shape=jax.Shap...  191 us
    transpose x1, local copies, waits for them, and re-layouts, in_one_kernel(): return jnp.transpose(out, (0, 2, 1, 3))  6.79 us
    unnamed x1, local copies, waits for them, and re-layouts  4.53 us

profile of v3, /device:TPU:9, one launch (start us, length us, event | category | flops | bytes accessed | tf_op | source)
XLA Modules:
  0.0 202.3 jit_solution(17322581594127732975)
XLA Ops:
  0.0 4.5 %copy.6 = bf16[3,256,2,1024]{3,1,2,0:T(8,128)(2,1)} copy(bf16[3,256,2,1024]{3,2,1,0:T(2,128)(2,1)} %param.2) | data formatting | bytes 6291456 | tf_op args[0]
  4.5 191.0 %shard_map.28 = bf16[3,2,256,1024]{3,2,1,0:T(8,128)(2,1)} custom-call(bf16[3,2,256,1024]{3,2,1,0:T(8,128)(2,1)} %bitcast.5, bf16[1024,1024]{1,0:T(8,128)(2,1)} %m_ref.1), custom_call_target="tpu_custom_call" | custom-call | tf_op jit(solution)/shard_map/pallas_call | solution.py:466
  195.5 6.8 %copy.4 = bf16[3,256,2,1024]{3,2,1,0:T(2,128)(2,1)} copy(bf16[3,256,2,1024]{3,1,2,0:T(8,128)(2,1)} %bitcast.4) | data formatting | bytes 6291456 | tf_op jit(solution)/shard_map/transpose | solution.py:512
